TPU v7x, 32 devices: a whole 2x2x4 slice. The times are simulated.
32 devices in a mesh: node: 16 (over z, x, core), grp: 2 (over y).
Axes of the slice: x: 2, y: 2, z: 4, core: 2. Of those that a mesh axis runs over, the one named last changes fastest.
Arguments:
- samples: bfloat16 [16384, 2048], P(('node', 'grp')), may hold values from -6 to 6
- diag_block: bfloat16 [16384, 1024], P(('node', 'grp')), may hold values from -0.1875 to 0.1875
- test_matrix: bfloat16 [16384, 2048], P('node'), may hold values from -6 to 6
- coeffs: bfloat16 [16384, 256], P(('node', 'grp')), may hold values from -0.1875 to 0.1875
- cross: bfloat16 [4096, 256], P('node'), may hold values from -0.375 to 0.375
- skeleton: int32 [16, 256], P('node'), may hold values from 0 to 1023, as said below
- counts: int32 [16], P('node'), may hold values from 64 to 256, as said below
- parent_slot: int32 [16], P('node'), may hold values from 0 to 1, as said below
Outputs:
- generators: bfloat16 [4096, 2048], P(('node', 'grp'))
- parent_samples: float32 [8192, 2048], P(('node', 'grp'))
Inputs may be any that keep to these rules, and one draw needn't show every extreme that they name: Each row holds 256 distinct rows of the node; the first counts of them are its skeleton, the rest are ignored. `counts`: some node has exactly 256. `parent_slot`: two siblings hold different values.
All inputs are finite; a program needn't handle non-finite values.
Results may differ from a plain program's by a relative error of at most 0.006.
Values may be sent and summed in bfloat16 or wider, within the bound.
No kernel may reach another device: no remote copies, remote signals or barrier semaphores. Data moves between devices by JAX's collectives and lax.ppermute only.
A program may use at most 64 MiB of HBM per device.

v0:
```python
import jax
import jax.numpy as jnp
from jax import lax
from jax.sharding import PartitionSpec as P

SIB_BIT = 2


def from_partner(block, axis, distance):
    count = lax.axis_size(axis)
    route = []
    for low in range(count):
        high = low | 1 << distance
        if high != low and high < count:
            route += [(low, high), (high, low)]
    return lax.ppermute(block, axis, route)


def local(samples, diag_block, test_matrix, coeffs, cross, skeleton, counts, parent_slot):
    group = lax.axis_index("grp")
    half_rows = samples.shape[0]
    skel_cap = cross.shape[1]
    share_rows = skel_cap // 2
    own_tests = lax.dynamic_slice_in_dim(test_matrix, group * half_rows, half_rows, 0)
    offdiag = (
        samples.astype(jnp.float32)
        - jnp.dot(diag_block, test_matrix, preferred_element_type=jnp.float32)
    ).astype(jnp.bfloat16)
    chosen = skeleton[0] - group * half_rows
    picker = (chosen[:, None] == jnp.arange(half_rows)[None, :]).astype(jnp.bfloat16)
    skel_part = jnp.dot(picker, offdiag, preferred_element_type=jnp.float32)
    gen_part = lax.dot_general(
        coeffs, own_tests, (((0,), (0,)), ((), ())), preferred_element_type=jnp.float32
    )
    gen_part = gen_part + jnp.dot(picker, own_tests, preferred_element_type=jnp.float32)
    live_slots = (jnp.arange(skel_cap) < counts[0])[:, None]
    own_slot = parent_slot[0]
    skel_sum, gen_sum = (
        lax.psum(skel_part.astype(jnp.bfloat16), "grp").astype(jnp.float32),
        lax.psum(gen_part.astype(jnp.bfloat16), "grp").astype(jnp.float32),
    )
    generator = jnp.where(live_slots, gen_sum, 0.0).astype(jnp.bfloat16)
    partner_gen = from_partner(generator, "node", SIB_BIT)
    parent = jnp.where(
        live_slots, skel_sum - jnp.dot(cross, partner_gen, preferred_element_type=jnp.float32), 0.0
    )
    partner_parent = from_partner(parent.astype(jnp.bfloat16), "node", SIB_BIT).astype(parent.dtype)
    gen_rows = lax.dynamic_slice_in_dim(generator, group * share_rows, share_rows, 0)
    block = jnp.where(own_slot == group, parent, partner_parent)
    return (gen_rows, block)


def solution(mesh):
    return jax.shard_map(
        local,
        mesh=mesh,
        in_specs=(
            P(("node", "grp"), None),
            P(("node", "grp"), None),
            P("node", None),
            P(("node", "grp"), None),
            P("node", None),
            P("node", None),
            P("node"),
            P("node"),
        ),
        out_specs=(P(("node", "grp"), None), P(("node", "grp"), None)),
        check_vma=False,
    )
```

profile of v0, /device:TPU:0, one launch (start us, length us, event | category | flops | bytes accessed | tf_op | source)
XLA Modules:
  0.0 149.8 jit_solution(7721908746787562983)
XLA Ops:
  7.2 0.0 copy-start
  7.2 0.0 all-reduce.3.cloned.1.call-start
  7.2 0.8 broadcast_subtract_fusion
  8.0 0.0 copy-start.2
  8.0 2.5 %convolution_bitcast_fusion.1 = f32[256,2048]{0,1:T(8,128)S(1)} fusion(bf16[512,256]{1,0:T(8,128)(2,1)} %param.11, bf16[1024,2048]{1,0:T(8,128)(2,1)} %param.10, s32[]{:T(128)S(6)} %select_n.21), kind=kOutput, calls=%fused_computation.3 | convolution fusion | flops 536870912 | bytes 4456452 | tf_op jit(solution)/shard_map/dot_general | solution.py:32
  10.5 0.4 copy-done.2
  10.9 0.0 copy-start.5
  10.9 2.0 %fusion.2 = bf16[256,2048]{0,1:T(8,128)(2,1)} fusion(f32[256,2048]{0,1:T(8,128)S(1)} %convolution_bitcast_fusion.1, bf16[1024,2048]{1,0:T(8,128)(2,1)S(1)} %copy-done.2, s32[]{:T(128)S(6)} %select_n.21, s32[256]{0:T(256)S(1)} %bitcast.18), kind=kOutput, calls=%fused_computation.6 | convolution fusion | flops 538050560 | bytes 5243908 | tf_op jit(solution)/shard_map/dot_general | solution.py:35
  12.9 0.0 copy-done
  12.9 0.0 copy-done.5
  12.9 6.1 %convolution_convert_fusion = bf16[256,2048]{0,1:T(8,128)(2,1)} fusion(bf16[512,2048]{1,0:T(8,128)(2,1)S(1)} %copy-done.5, bf16[512,1024]{1,0:T(8,128)(2,1)S(1)} %copy-done, bf16[1024,2048]{1,0:T(8,128)(2,1)} %param.10, s32[256]{0:T(256)S(1)} %bitcast.19), kind=kOutput, calls=%fused_computation.7 | convolution fusion | flops 2688155648 | bytes 8389632 | tf_op jit(solution)/shard_map/dot_general | solution.py:31
  19.1 0.0 copy-start.4
  19.1 0.0 all-reduce.3.cloned.1.call-update
  19.8 65.3 %all-reduce.3.cloned.1.call-done = (bf16[256,2048]{0,1:T(8,128)(2,1)}, bf16[256,2048]{0,1:T(8,128)(2,1)}) async-done(((bf16[256,2048]{0,1:T(8,128)(2,1)}, bf16[256,2048]{0,1:T(8,128)(2,1)}), (bf16[256,2048]{0,1:T(8,128)(2,1)}, bf16[256,2048]{0,1:T(8,128)(2,1)})) %all-reduce.3.cloned.1.call-update) | async-done | bytes 2097168 | tf_op jit(solution)/shard_map/psum | solution.py:40
  85.0 0.0 copy-start.3
  85.0 1.5 %select_convert_fusion = bf16[256,2048]{0,1:T(8,128)(2,1)S(1)} fusion(bf16[256,2048]{0,1:T(8,128)(2,1)} %get-tuple-element.4, pred[256]{0:T(512)(128)(4,1)S(1)} %iota_compare_fusion.3), kind=kLoop, calls=%fused_computation.9 | loop fusion | flops 1572864 | bytes 2097408 | tf_op jit(solution)/shard_map/convert_element_type | solution.py:42
  86.6 0.0 copy-start.1
  86.6 1.6 %collective-permute-start = (bf16[256,2048]{0,1:T(8,128)(2,1)S(1)}, bf16[256,2048]{0,1:T(8,128)(2,1)S(1)}, u32[]{:S(2)}, u32[]{:S(2)}) collective-permute-start(bf16[256,2048]{0,1:T(8,128)(2,1)S(1)} %select_convert_fusion), channel_id=1, source_target_pairs={{0,8},{8,0},{2,10},{10,2},{4,12},{12,4},{6,14},{14,6},{16,24},{24,... | collective-permute-start | bytes 3145736 | tf_op jit(solution)/shard_map/ppermute | solution.py:16
  88.1 23.4 %collective-permute-done = bf16[256,2048]{0,1:T(8,128)(2,1)S(1)} collective-permute-done((bf16[256,2048]{0,1:T(8,128)(2,1)S(1)}, bf16[256,2048]{0,1:T(8,128)(2,1)S(1)}, u32[]{:S(2)}, u32[]{:S(2)}) %collective-permute-start) | collective-permute-done | bytes 1048608 | tf_op jit(solution)/shard_map/ppermute | solution.py:16
  111.5 0.0 copy-done.4
  111.5 0.0 copy-done.3
  111.5 1.4 fusion.9
  113.0 0.0 copy-done.1
  113.0 1.5 collective-permute-start.1
  115.1 1.9 %constant_dynamic-slice_fusion = bf16[128,2048]{0,1:T(8,128)(2,1)} fusion(bf16[256,2048]{0,1:T(8,128)(2,1)} %copy-done.1, s32[]{:T(128)S(6)} %select_n.23), kind=kLoop, calls=%fused_computation.18 | loop fusion | bytes 1048580 | tf_op jit(solution)/shard_map/dynamic_slice | solution.py:48
  117.0 2.0 %copy.12 = bf16[128,2048]{1,0:T(8,128)(2,1)} copy(bf16[128,2048]{0,1:T(8,128)(2,1)} %constant_dynamic-slice_fusion) | data formatting | bytes 1048576
  119.1 18.3 %collective-permute-done.1 = bf16[256,2048]{0,1:T(8,128)(2,1)} collective-permute-done((bf16[256,2048]{0,1:T(8,128)(2,1)}, bf16[256,2048]{0,1:T(8,128)(2,1)}, u32[]{:S(2)}, u32[]{:S(2)}) %collective-permute-start.1) | collective-permute-done | bytes 1048608 | tf_op jit(solution)/shard_map/ppermute | solution.py:16
  137.3 2.8 %convert_select_fusion = f32[256,2048]{0,1:T(8,128)} fusion(f32[256,2048]{0,1:T(8,128)S(1)} %get-tuple-element.7, bf16[256,2048]{0,1:T(8,128)(2,1)} %collective-permute-done.1, pred[]{:T(512)S(6)} %eq.19), kind=kLoop, calls=%fused_computation.8 | loop fusion | flops 1048576 | bytes 5242881 | tf_op jit(solution)/shard_map/jit(_where)/select_n | solution.py:49
  140.1 2.9 %copy.13 = f32[256,2048]{1,0:T(8,128)} copy(f32[256,2048]{0,1:T(8,128)} %convert_select_fusion) | data formatting | bytes 4194304
  (1 shorter events, 0.0 us)
Async XLA Ops:
  7.2 5.8 %copy-start = (bf16[512,1024]{1,0:T(8,128)(2,1)S(1)}, bf16[512,1024]{1,0:T(8,128)(2,1)}, u32[]{:S(2)}) copy-start(bf16[512,1024]{1,0:T(8,128)(2,1)} %param.9) | copy-start | bytes 3145732
  7.2 77.9 %all-reduce.3.cloned.1.call-start = ((), (), s32[]{:S(2)}) async-start(), calls=%async_computation | async-start | bytes 4194304 | tf_op jit(solution)/shard_map/psum | solution.py:40
  8.0 2.9 %copy-start.2 = (bf16[1024,2048]{1,0:T(8,128)(2,1)S(1)}, bf16[1024,2048]{1,0:T(8,128)(2,1)}, u32[]{:S(2)}) copy-start(bf16[1024,2048]{1,0:T(8,128)(2,1)} %param.10) | copy-start | bytes 12582916
  10.9 2.0 %copy-start.5 = (bf16[512,2048]{1,0:T(8,128)(2,1)S(1)}, bf16[512,2048]{1,0:T(8,128)(2,1)}, u32[]{:S(2)}) copy-start(bf16[512,2048]{1,0:T(8,128)(2,1)} %param.8) | copy-start | bytes 6291460
  19.1 92.5 %copy-start.4 = (bf16[256,256]{1,0:T(8,128)(2,1)S(1)}, bf16[256,256]{1,0:T(8,128)(2,1)}, u32[]{:S(2)}) copy-start(bf16[256,256]{1,0:T(8,128)(2,1)} %param.12) | copy-start | bytes 393220
  85.0 26.5 %copy-start.3 = (bf16[256,2048]{0,1:T(8,128)(2,1)S(1)}, bf16[256,2048]{0,1:T(8,128)(2,1)}, u32[]{:S(2)}) copy-start(bf16[256,2048]{0,1:T(8,128)(2,1)} %get-tuple-element.5) | copy-start | bytes 3145732
  86.6 26.4 %copy-start.1 = (bf16[256,2048]{0,1:T(8,128)(2,1)}, bf16[256,2048]{0,1:T(8,128)(2,1)S(1)}, u32[]{:S(2)}) copy-start(bf16[256,2048]{0,1:T(8,128)(2,1)S(1)} %select_convert_fusion) | copy-start | bytes 3145732
  86.6 25.0 %collective-permute-start = (bf16[256,2048]{0,1:T(8,128)(2,1)S(1)}, bf16[256,2048]{0,1:T(8,128)(2,1)S(1)}, u32[]{:S(2)}, u32[]{:S(2)}) collective-permute-start(bf16[256,2048]{0,1:T(8,128)(2,1)S(1)} %select_convert_fusion), channel_id=1, source_target_pairs={{0,8},{8,0},{2,10},{10,2},{4,12},{12,4},{6,14},{14,6},{16,24},{24,... | collective-permute-start | bytes 3145736 | tf_op jit(solution)/shard_map/ppermute | solution.py:16
  113.0 24.3 %collective-permute-start.1 = (bf16[256,2048]{0,1:T(8,128)(2,1)}, bf16[256,2048]{0,1:T(8,128)(2,1)}, u32[]{:S(2)}, u32[]{:S(2)}) collective-permute-start(bf16[256,2048]{0,1:T(8,128)(2,1)} %get-tuple-element.6), channel_id=1, source_target_pairs={{0,8},{8,0},{2,10},{10,2},{4,12},{12,4},{6,14},{14,6},{16,24},{24,... | collective-permute-start | bytes 3145736 | tf_op jit(solution)/shard_map/ppermute | solution.py:16
Sparse Core Ops, SparseCore 0:
  19.2 65.7 all-reduce.2
where the time goes:
time: 150 us
  waiting for transfers between devices  107 us (71%)
  between operations  15.4 us (10%)
  matrix products  12.1 us (8%)
  local copies, waits for them, and re-layouts  7.25 us (5%)
  other arithmetic  5.03 us (3%)
  starting transfers between devices  3.07 us (2%)
    psum x1, waiting for transfers between devices, local(): lax.psum(gen_part.astype(jnp.bfloat16), 'grp').astype(jnp.float32)  65.3 us
    ppermute x2, waiting for transfers between devices, from_partner(): return lax.ppermute(block, axis, route)  41.7 us
    dot_general x1, matrix products, local(): skel_part = jnp.dot(picker, offdiag, preferred_element_type=jnp.float32)  6.12 us
    unnamed x14, local copies, waits for them, and re-layouts  5.35 us
    ppermute x2, starting transfers between devices, from_partner(): return lax.ppermute(block, axis, route)  3.03 us
  transfers between devices with their start and end apart: 3, of which 3 were waited for; matrix products, arithmetic and copies ran while one was open for 3% of the time, Pallas kernels for 0%

commit v1 on v0

v1 whole, which is shorter than its diff:
```python
import functools

import jax
import jax.numpy as jnp
from jax import lax
from jax.experimental import pallas as pl
from jax.experimental.pallas import tpu as pltpu
from jax.sharding import PartitionSpec as P

SIB_BIT = 2
CHUNKS = 4
BLOCK = 256
F32, BF16 = jnp.float32, jnp.bfloat16

VMEM = pl.BlockSpec(memory_space=pltpu.VMEM)
SMEM = pl.BlockSpec(memory_space=pltpu.SMEM)
ANY = pl.BlockSpec(memory_space=pl.ANY)


def swap(block, axis, distance):
    count = lax.axis_size(axis)
    route = []
    for low in range(count):
        high = low | 1 << distance
        if high != low and high < count:
            route += [(low, high), (high, low)]
    return lax.ppermute(block, axis, route)


def call(body, outs, in_specs, out_specs, operands, scratch=(), flops=0, moved=0, alias=None):
    return pl.pallas_call(
        body,
        out_shape=outs,
        in_specs=in_specs,
        out_specs=out_specs,
        scratch_shapes=list(scratch),
        input_output_aliases=alias or {},
        compiler_params=pltpu.CompilerParams(vmem_limit_bytes=40 * 2**20),
        cost_estimate=pl.CostEstimate(flops=flops, bytes_accessed=moved, transcendentals=0),
    )(*operands)


def hot_rows(skel_ref, first, rows, live):
    slots = skel_ref.shape[1]
    down = jnp.broadcast_to(skel_ref[...], (128, slots)).T
    alive = lax.broadcasted_iota(jnp.int32, (slots, 128), 0) < live
    down = jnp.where(alive, down - first, -1)
    lane = lax.broadcasted_iota(jnp.int32, (slots, 128), 1)
    parts = [jnp.where(down == lane + at, 1.0, 0.0).astype(BF16) for at in range(0, rows, 128)]
    return jnp.concatenate(parts, axis=1)


def mm(a, b):
    return jnp.dot(a, b, preferred_element_type=F32)


def mmt(a, b):
    return lax.dot_general(a, b, (((0,), (0,)), ((), ())), preferred_element_type=F32)


def first_body(slot_ref, count_ref, skel_ref, cross_ref, coeffs_ref, diag_ref, samples_ref, tests_ref,
               message_ref, cross_out_ref, hot_ref, diag_rows_ref,
               diag_buf, samples_buf, tests_buf, sems):
    group = lax.axis_index("grp")
    half, cap = coeffs_ref.shape
    width = samples_buf.shape[1]
    owner = slot_ref[0] == group
    copies = [
        pltpu.make_async_copy(diag_ref, diag_buf, sems.at[0]),
        pltpu.make_async_copy(samples_ref.at[:, pl.ds(0, width)], samples_buf, sems.at[1]),
        pltpu.make_async_copy(tests_ref.at[:, pl.ds(0, width)], tests_buf, sems.at[2]),
    ]
    for copy in copies:
        copy.start()
    live = count_ref[0]
    alive = lax.broadcasted_iota(jnp.int32, (cap, cap), 0) < live
    cross_out_ref[...] = jnp.where(alive, cross_ref[...].astype(F32), 0.0).astype(BF16)
    hot = hot_rows(skel_ref, group * half, half, live)
    hot_ref[...] = hot
    copies[0].wait()
    diag_rows = (-mm(hot, diag_buf[...])).astype(BF16)
    diag_rows_ref[...] = diag_rows
    copies[1].wait()
    copies[2].wait()

    @pl.when(owner)
    def _():
        message_ref[...] = coeffs_ref[...]

    @pl.when(jnp.logical_not(owner))
    def _():
        for at in range(0, width, cap):
            part = mm(hot, samples_buf[:, at:at + cap]) + mm(diag_rows, tests_buf[:, at:at + cap])
            message_ref[pl.ds(at, cap), :] = part.astype(BF16)


def skel_body(hot_ref, diag_rows_ref, samples_ref, tests_ref, *rest):
    outs = rest[:CHUNKS]
    samples_buf, tests_buf, sems = rest[CHUNKS:]
    width = outs[0].shape[1]
    copies = []
    for i in range(CHUNKS):
        cut = pl.ds(i * width, width)
        pair = (pltpu.make_async_copy(samples_ref.at[:, cut], samples_buf.at[:, cut], sems.at[0, i]),
                pltpu.make_async_copy(tests_ref.at[:, cut], tests_buf.at[:, cut], sems.at[1, i]))
        for copy in pair:
            copy.start()
        copies.append(pair)
    for i in range(CHUNKS):
        for copy in copies[i]:
            copy.wait()
        for at in range(0, width, BLOCK):
            cut = slice(i * width + at, i * width + at + BLOCK)
            part = mm(hot_ref[...], samples_buf[:, cut]) + mm(diag_rows_ref[...], tests_buf[:, cut])
            outs[i][:, at:at + BLOCK] = part.astype(BF16)


def send_body(index, slot_ref, count_ref, skel_ref, coeffs_ref, other_ref, own_ref, got_ref, tests_ref, out_ref):
    group = lax.axis_index("grp")
    half, cap = coeffs_ref.shape
    width = out_ref.shape[1]
    owner = slot_ref[0] == group

    @pl.when(owner)
    def _():
        if index == 0:
            for at in range(0, width, cap):
                out_ref[:, at:at + cap] = own_ref[:, at:at + cap] + got_ref[at:at + cap, :]
        else:
            out_ref[...] = own_ref[...] + got_ref[...]

    @pl.when(jnp.logical_not(owner))
    def _():
        live = count_ref[0]
        hot = hot_rows(skel_ref, 0, 2 * half, live)
        alive = lax.broadcasted_iota(jnp.int32, (cap, BLOCK), 0) < live
        mine = pl.ds(pl.multiple_of(group * half, half), half)
        theirs = pl.ds(pl.multiple_of((1 - group) * half, half), half)
        for at in range(0, width, BLOCK):
            cut = slice(index * width + at, index * width + at + BLOCK)
            part = (mmt(coeffs_ref[...], tests_ref[mine, cut]) + mmt(other_ref[...], tests_ref[theirs, cut])
                    + mm(hot, tests_ref[:, cut]))
            out_ref[:, at:at + BLOCK] = jnp.where(alive, part, 0.0).astype(BF16)


def generator_body(count_ref, skel_ref, coeffs_ref, other_ref, tests_ref, out_ref):
    group = lax.axis_index("grp")
    half = coeffs_ref.shape[0]
    share, width = out_ref.shape
    live = count_ref[0]
    hot = hot_rows(skel_ref, 0, 2 * half, live)
    hot = jnp.where(group == 0, hot[:share].astype(F32), hot[share:].astype(F32)).astype(BF16)
    coeffs = jnp.where(group == 0, coeffs_ref[:, :share].astype(F32), coeffs_ref[:, share:].astype(F32)).astype(BF16)
    alive = lax.broadcasted_iota(jnp.int32, (share, BLOCK), 0) + group * share < live
    mine = pl.ds(pl.multiple_of(group * half, half), half)
    theirs = pl.ds(pl.multiple_of((1 - group) * half, half), half)
    for at in range(0, width, BLOCK):
        cut = slice(at, at + BLOCK)
        part = (mmt(coeffs, tests_ref[mine, cut]) + mmt(other_ref[...], tests_ref[theirs, cut])
                + mm(hot, tests_ref[:, cut]))
        out_ref[:, cut] = jnp.where(alive, part, 0.0).astype(BF16)


def parent_body(index, slot_ref, cross_ref, cross_got_ref, sent_ref, got_ref, *rest):
    out_ref, buf, sem = rest[-3:]
    group = lax.axis_index("grp")
    width = sent_ref.shape[1]
    owner = slot_ref[0] == group

    @pl.when(owner)
    def _():
        buf[...] = sent_ref[...].astype(F32) - mm(cross_ref[...], got_ref[...])

    @pl.when(jnp.logical_not(owner))
    def _():
        buf[...] = got_ref[...].astype(F32) - mm(cross_got_ref[...], sent_ref[...])

    copy = pltpu.make_async_copy(buf, out_ref.at[:, pl.ds(index * width, width)], sem)
    copy.start()
    copy.wait()


def local(samples, diag_block, test_matrix, coeffs, cross, skeleton, counts, parent_slot):
    half, cap = coeffs.shape
    rows, cols = test_matrix.shape
    share = cap // 2
    width = cols // CHUNKS
    group = lax.axis_index("grp")
    like = jax.ShapeDtypeStruct

    message, cross_live, hot, diag_rows = call(
        first_body,
        (like((half, cap), BF16), like((cap, cap), BF16), like((cap, half), BF16), like((cap, rows), BF16)),
        [SMEM, SMEM, VMEM, VMEM, VMEM, ANY, ANY, ANY],
        (VMEM,) * 4,
        (parent_slot, counts, skeleton, cross, coeffs, diag_block, samples, test_matrix),
        [pltpu.VMEM((half, rows), BF16), pltpu.VMEM((half, width), BF16), pltpu.VMEM((rows, width), BF16),
         pltpu.SemaphoreType.DMA((3,))],
        flops=2 * cap * rows * (half + width), moved=2 * (half * rows + (half + rows) * width),
    )
    got = [swap(message, "grp", 0)]
    cross_got = swap(cross_live, "node", SIB_BIT)
    own = call(
        skel_body,
        [like((cap, width), BF16)] * CHUNKS,
        [VMEM, VMEM, ANY, ANY],
        [VMEM] * CHUNKS,
        (hot, diag_rows, samples, test_matrix),
        [pltpu.VMEM((half, cols), BF16), pltpu.VMEM((rows, cols), BF16), pltpu.SemaphoreType.DMA((2, CHUNKS))],
        flops=2 * cap * (rows + half) * cols, moved=2 * (half + rows + cap) * cols,
    )
    got += [swap(own[i], "grp", 0) for i in range(1, CHUNKS)]
    other_share = swap(lax.dynamic_slice_in_dim(coeffs, (1 - group) * share, share, 1), "grp", 0)
    out = None
    for i in range(CHUNKS):
        sent = call(
            functools.partial(send_body, i),
            like((cap, width), BF16),
            [SMEM, SMEM, VMEM, VMEM, VMEM, VMEM, VMEM, VMEM],
            VMEM,
            (parent_slot, counts, skeleton, coeffs, got[0], own[i], got[i], test_matrix),
            flops=4 * cap * rows * width, moved=2 * (rows + 2 * cap) * width,
        )
        arrived = swap(sent, "node", SIB_BIT)
        out = call(
            functools.partial(parent_body, i),
            like((cap, cols), F32),
            [SMEM, VMEM, VMEM, VMEM, VMEM] + ([] if out is None else [ANY]),
            ANY,
            (parent_slot, cross_live, cross_got, sent, arrived) + (() if out is None else (out,)),
            [pltpu.VMEM((cap, width), F32), pltpu.SemaphoreType.DMA],
            flops=2 * cap * cap * width, moved=8 * cap * width,
            alias=None if out is None else {5: 0},
        )
    generators = call(
        generator_body,
        like((share, cols), BF16),
        [SMEM, VMEM, VMEM, VMEM, VMEM],
        VMEM,
        (counts, skeleton, coeffs, other_share, test_matrix),
        flops=4 * share * rows * cols, moved=2 * (rows + share) * cols,
    )
    return generators, out


def solution(mesh):
    return jax.shard_map(
        local,
        mesh=mesh,
        in_specs=(
            P(("node", "grp"), None),
            P(("node", "grp"), None),
            P("node", None),
            P(("node", "grp"), None),
            P("node", None),
            P("node", None),
            P("node"),
            P("node"),
        ),
        out_specs=(P(("node", "grp"), None), P(("node", "grp"), None)),
        check_vma=False,
    )
```

time: 150 us -> 55.3 us (0.37)
  waiting for transfers between devices: 107 us -> 12.8 us
  starting transfers between devices: 3.07 us -> 19.6 us
  between operations: 15.4 us -> 2.06 us
  matrix products: 12.1 us -> 0 us
  Pallas kernels: 0 us -> 10.7 us
  other arithmetic: 5.03 us -> 0 us
  local copies, waits for them, and re-layouts: 7.25 us -> 9.75 us
    psum x1 -> x0, waiting for transfers between devices: 65.3 us -> none  [local(): lax.psum(gen_part.astype(jnp.bfloat16), 'grp').astype(jnp.float32)]
    ppermute x2 -> x10, waiting for transfers between devices: 41.7 us -> 12.8 us  [swap(): return lax.ppermute(block, axis, route)]
    ppermute x2 -> x10, starting transfers between devices: 3.03 us -> 19.6 us  [swap(): return lax.ppermute(block, axis, route)]
    dot_general x4 -> x0, matrix products: 12.1 us -> none  [the longest x1 6.12 us: local(): skel_part = jnp.dot(picker, offdiag, preferred_element_type=jnp.float32)]
    pallas_call x0 -> x11, Pallas kernels: none -> 10.7 us  [call(): pl.pallas_call(body, out_shape=outs, in_specs=in_specs, out_specs=out_spe...]
    unnamed x14 -> x24, local copies, waits for them, and re-layouts: 5.35 us -> 9.74 us
    select_n x1 -> x0, other arithmetic: 2.76 us -> none  [local(): block = jnp.where(own_slot == group, parent, partner_parent)]
    dynamic_slice x1, local copies, waits for them, and re-layouts: 1.9 us -> 0.01 us  [local(): lax.dynamic_slice_in_dim(coeffs, (1 - group) * share, share, 1)]
  transfers between devices with their start and end apart: 3 -> 10, of which waited for: 3 -> 4; matrix products, arithmetic and copies ran while one was open for 3% -> 0% of each run, Pallas kernels for 0% -> 16%
where the time goes in v1:
time: 55.3 us; the launch traced here: 55 us
  starting transfers between devices  19.6 us (35%)
  waiting for transfers between devices  12.8 us (23%)
  Pallas kernels  10.7 us (19%)
  local copies, waits for them, and re-layouts  9.75 us (18%)
  between operations  2.06 us (4%)
    ppermute x10, starting transfers between devices, swap(): return lax.ppermute(block, axis, route)  19.6 us
    ppermute x10, waiting for transfers between devices, swap(): return lax.ppermute(block, axis, route)  12.8 us
    pallas_call x11, Pallas kernels, call(): pl.pallas_call(body, out_shape=outs, in_specs=in_specs, out_specs=out_spe...  10.7 us
    unnamed x24, local copies, waits for them, and re-layouts  9.74 us
  transfers between devices with their start and end apart: 10, of which 4 were waited for; matrix products, arithmetic and copies ran while one was open for 0% of the time, Pallas kernels for 16%

profile of v1, /device:TPU:0, one launch (start us, length us, event | category | flops | bytes accessed | tf_op | source)
XLA Modules:
  0.0 55.0 jit_solution(12077334606329218348)
XLA Ops:
  1.9 0.0 copy-start
  1.9 2.2 %copy-done = bf16[1024,2048]{1,0:T(8,128)(2,1)S(1)} copy-done((bf16[1024,2048]{1,0:T(8,128)(2,1)S(1)}, bf16[1024,2048]{1,0:T(8,128)(2,1)}, u32[]{:S(2)}) %copy-start) | copy-done | bytes 4194328
  4.1 0.0 copy-start.4
  4.1 0.9 %copy-done.4 = bf16[512,256]{1,0:T(8,128)(2,1)S(1)} copy-done((bf16[512,256]{1,0:T(8,128)(2,1)S(1)}, bf16[512,256]{1,0:T(8,128)(2,1)}, u32[]{:S(2)}) %copy-start.4) | copy-done | bytes 262168
  5.1 0.0 copy-start.6
  5.1 1.6 %copy-done.6 = bf16[512,2048]{1,0:T(8,128)(2,1)S(1)} copy-done((bf16[512,2048]{1,0:T(8,128)(2,1)S(1)}, bf16[512,2048]{1,0:T(8,128)(2,1)}, u32[]{:S(2)}) %copy-start.6) | copy-done | bytes 2097176
  6.7 0.0 copy-start.8
  6.7 1.2 %copy-done.8 = bf16[512,1024]{1,0:T(8,128)(2,1)S(1)} copy-done((bf16[512,1024]{1,0:T(8,128)(2,1)S(1)}, bf16[512,1024]{1,0:T(8,128)(2,1)}, u32[]{:S(2)}) %copy-start.8) | copy-done | bytes 1048600
  7.9 0.0 copy-start.9
  7.9 0.9 %copy-done.9 = bf16[256,256]{1,0:T(8,128)(2,1)S(1)} copy-done((bf16[256,256]{1,0:T(8,128)(2,1)S(1)}, bf16[256,256]{1,0:T(8,128)(2,1)}, u32[]{:S(2)}) %copy-start.9) | copy-done | bytes 131096
  8.8 0.0 copy-start.10
  8.8 0.7 %copy-done.10 = s32[1,256]{1,0:T(1,128)S(1)} copy-done((s32[1,256]{1,0:T(1,128)S(1)}, s32[1,256]{1,0:T(1,128)}, u32[]{:S(2)}) %copy-start.10) | copy-done | bytes 1048
  9.5 0.0 copy-start.1
  9.5 0.0 copy-start.7
  9.5 0.9 %shard_map.96 = (bf16[512,256]{1,0:T(8,128)(2,1)S(1)}, bf16[256,256]{1,0:T(8,128)(2,1)S(1)}, bf16[256,512]{1,0:T(8,128)(2,1)S(1)}, bf16[256,1024]{1,0:T(8,128)(2,1)S(1)}) custom-call(s32[1]{0:T(128)S(6)} %copy.17.slot_ref, s32[1]{0:T(128)S(6)} %copy.16.count_ref, s32[1,256]{1,0:T(1,128)S(1)} %copy-done.10, bf16[256,256]{1,0:T(8,128)(2,1)S(1)} %copy-done.9, ...), custom_call_target="tpu_custom_call" | custom-call | flops 536870912 | bytes 2621440 | tf_op jit(solution)/shard_map/pallas_call | solution.py:31
  10.4 3.6 %collective-permute-start.2 = (bf16[512,256]{1,0:T(8,128)(2,1)S(1)}, bf16[512,256]{1,0:T(8,128)(2,1)S(1)}, u32[]{:S(2)}, u32[]{:S(2)}) collective-permute-start(bf16[512,256]{1,0:T(8,128)(2,1)S(1)} %get-tuple-element.11), channel_id=1, source_target_pairs={{0,1},{1,0},{2,3},{3,2},{4,5},{5,4},{6,7},{7,6},{8,9},{9,8},{10,11... | collective-permute-start | bytes 786440 | tf_op jit(solution)/shard_map/ppermute | solution.py:27
  14.0 0.0 copy-done.1
  14.0 0.0 copy-done.7
  14.0 3.2 %shard_map.97 = (bf16[256,512]{1,0:T(8,128)(2,1)S(1)}, bf16[256,512]{1,0:T(8,128)(2,1)S(1)}, bf16[256,512]{1,0:T(8,128)(2,1)S(1)}, bf16[256,512]{1,0:T(8,128)(2,1)S(1)}) custom-call(bf16[256,512]{1,0:T(8,128)(2,1)S(1)} %get-tuple-element.12.hot_ref, bf16[256,1024]{1,0:T(8,128)(2,1)S(1)} %get-tuple-element.13.diag_rows_ref, bf16[512,2048]{1,0:T(8,128)(2,1)S(1)} %copy-done.7, ...), custom_call_target="tpu_custom_call" | custom-call | flops 1610612736 | bytes 7340032 | tf_op jit(solution)/shard_map/pallas_call | solution.py:31
  17.3 1.4 %collective-permute-start.7 = (bf16[256,512]{1,0:T(8,128)(2,1)S(1)}, bf16[256,512]{1,0:T(8,128)(2,1)S(1)}, u32[]{:S(2)}, u32[]{:S(2)}) collective-permute-start(bf16[256,512]{1,0:T(8,128)(2,1)S(1)} %get-tuple-element.16.own_ref), channel_id=1, source_target_pairs={{0,1},{1,0},{2,3},{3,2},{4,5},{5,4},{6,7},{7,6},{8,9},{9,8},{10,11... | collective-permute-start | bytes 786440 | tf_op jit(solution)/shard_map/ppermute | solution.py:27
  18.6 0.7 %collective-permute-start.5 = (bf16[256,512]{1,0:T(8,128)(2,1)S(1)}, bf16[256,512]{1,0:T(8,128)(2,1)S(1)}, u32[]{:S(2)}, u32[]{:S(2)}) collective-permute-start(bf16[256,512]{1,0:T(8,128)(2,1)S(1)} %get-tuple-element.15.own_ref), channel_id=1, source_target_pairs={{0,1},{1,0},{2,3},{3,2},{4,5},{5,4},{6,7},{7,6},{8,9},{9,8},{10,11... | collective-permute-start | bytes 786440 | tf_op jit(solution)/shard_map/ppermute | solution.py:27
  19.4 1.3 %collective-permute-start.3 = (bf16[256,512]{1,0:T(8,128)(2,1)S(1)}, bf16[256,512]{1,0:T(8,128)(2,1)S(1)}, u32[]{:S(2)}, u32[]{:S(2)}) collective-permute-start(bf16[256,512]{1,0:T(8,128)(2,1)S(1)} %get-tuple-element.14.own_ref), channel_id=1, source_target_pairs={{0,1},{1,0},{2,3},{3,2},{4,5},{5,4},{6,7},{7,6},{8,9},{9,8},{10,11... | collective-permute-start | bytes 786440 | tf_op jit(solution)/shard_map/ppermute | solution.py:27
  20.6 0.0 copy-done.5
  20.7 0.8 %collective-permute-start = (bf16[512,128]{1,0:T(8,128)(2,1)S(1)}, bf16[512,128]{1,0:T(8,128)(2,1)S(1)}, u32[]{:S(2)}, u32[]{:S(2)}) collective-permute-start(bf16[512,128]{1,0:T(8,128)(2,1)S(1)} %constant_dynamic-slice_fusion), channel_id=1, source_target_pairs={{0,1},{1,0},{2,3},{3,2},{4,5},{5,4},{6,7},{7,6},{8,9},{9,8},{10,11... | collective-permute-start | bytes 393224 | tf_op jit(solution)/shard_map/ppermute | solution.py:27
  21.5 0.0 collective-permute-done.2.other_ref.got_ref
  21.5 0.0 copy-done.11
  21.5 2.2 %copy-done.2 = bf16[1024,2048]{1,0:T(8,128)(2,1)S(1)} copy-done((bf16[1024,2048]{1,0:T(8,128)(2,1)S(1)}, bf16[1024,2048]{1,0:T(8,128)(2,1)}, u32[]{:S(2)}) %copy-start.2) | copy-done | bytes 4194328
  23.7 2.4 %collective-permute-start.9 = (bf16[256,512]{1,0:T(8,128)(2,1)S(1)}, bf16[256,512]{1,0:T(8,128)(2,1)S(1)}, u32[]{:S(2)}, u32[]{:S(2)}) collective-permute-start(bf16[256,512]{1,0:T(8,128)(2,1)S(1)} %shard_map.101.sent_ref), channel_id=1, source_target_pairs={{0,8},{8,0},{2,10},{10,2},{4,12},{12,4},{6,14},{14,6},{16,24},{24,... | collective-permute-start | bytes 786440 | tf_op jit(solution)/shard_map/ppermute | solution.py:27
  26.1 0.6 %collective-permute-done.7.got_ref = bf16[256,512]{1,0:T(8,128)(2,1)S(1)} collective-permute-done((bf16[256,512]{1,0:T(8,128)(2,1)S(1)}, bf16[256,512]{1,0:T(8,128)(2,1)S(1)}, u32[]{:S(2)}, u32[]{:S(2)}) %collective-permute-start.7) | collective-permute-done | bytes 262176 | tf_op jit(solution)/shard_map/ppermute | solution.py:27
  26.7 2.8 %collective-permute-start.8 = (bf16[256,512]{1,0:T(8,128)(2,1)S(1)}, bf16[256,512]{1,0:T(8,128)(2,1)S(1)}, u32[]{:S(2)}, u32[]{:S(2)}) collective-permute-start(bf16[256,512]{1,0:T(8,128)(2,1)S(1)} %shard_map.100.sent_ref), channel_id=1, source_target_pairs={{0,8},{8,0},{2,10},{10,2},{4,12},{12,4},{6,14},{14,6},{16,24},{24,... | collective-permute-start | bytes 786440 | tf_op jit(solution)/shard_map/ppermute | solution.py:27
  29.5 2.8 %collective-permute-done.5.got_ref = bf16[256,512]{1,0:T(8,128)(2,1)S(1)} collective-permute-done((bf16[256,512]{1,0:T(8,128)(2,1)S(1)}, bf16[256,512]{1,0:T(8,128)(2,1)S(1)}, u32[]{:S(2)}, u32[]{:S(2)}) %collective-permute-start.5) | collective-permute-done | bytes 262176 | tf_op jit(solution)/shard_map/ppermute | solution.py:27
  32.3 0.0 copy-start.3
  32.3 2.8 %collective-permute-start.6 = (bf16[256,512]{1,0:T(8,128)(2,1)S(1)}, bf16[256,512]{1,0:T(8,128)(2,1)S(1)}, u32[]{:S(2)}, u32[]{:S(2)}) collective-permute-start(bf16[256,512]{1,0:T(8,128)(2,1)S(1)} %shard_map.99.sent_ref), channel_id=1, source_target_pairs={{0,8},{8,0},{2,10},{10,2},{4,12},{12,4},{6,14},{14,6},{16,24},{24,... | collective-permute-start | bytes 786440 | tf_op jit(solution)/shard_map/ppermute | solution.py:27
  35.2 2.7 %collective-permute-done.3.got_ref = bf16[256,512]{1,0:T(8,128)(2,1)S(1)} collective-permute-done((bf16[256,512]{1,0:T(8,128)(2,1)S(1)}, bf16[256,512]{1,0:T(8,128)(2,1)S(1)}, u32[]{:S(2)}, u32[]{:S(2)}) %collective-permute-start.3) | collective-permute-done | bytes 262176 | tf_op jit(solution)/shard_map/ppermute | solution.py:27
  37.9 2.8 %collective-permute-start.4 = (bf16[256,512]{1,0:T(8,128)(2,1)S(1)}, bf16[256,512]{1,0:T(8,128)(2,1)S(1)}, u32[]{:S(2)}, u32[]{:S(2)}) collective-permute-start(bf16[256,512]{1,0:T(8,128)(2,1)S(1)} %shard_map.98.sent_ref), channel_id=1, source_target_pairs={{0,8},{8,0},{2,10},{10,2},{4,12},{12,4},{6,14},{14,6},{16,24},{24,... | collective-permute-start | bytes 786440 | tf_op jit(solution)/shard_map/ppermute | solution.py:27
  40.8 0.0 collective-permute-done.other_ref
  40.8 1.0 %collective-permute-start.1 = (bf16[256,256]{1,0:T(8,128)(2,1)S(1)}, bf16[256,256]{1,0:T(8,128)(2,1)S(1)}, u32[]{:S(2)}, u32[]{:S(2)}) collective-permute-start(bf16[256,256]{1,0:T(8,128)(2,1)S(1)} %get-tuple-element.10.cross_ref), channel_id=1, source_target_pairs={{0,8},{8,0},{2,10},{10,2},{4,12},{12,4},{6,14},{14,6},{16,24},{24,... | collective-permute-start | bytes 393224 | tf_op jit(solution)/shard_map/ppermute | solution.py:27
  41.8 0.0 copy-done.3
  41.8 2.3 %shard_map.95 = bf16[128,2048]{1,0:T(8,128)(2,1)} custom-call(s32[1]{0:T(128)S(6)} %copy.16.count_ref, s32[1,256]{1,0:T(1,128)S(1)} %copy-done.11, bf16[512,256]{1,0:T(8,128)(2,1)S(1)} %copy-done.5, bf16[512,128]{1,0:T(8,128)(2,1)S(1)} %collective-permute-done.other_ref, bf16[1024,2048]{1,0:T(8,128)(2,1)S(1)} %copy-done.3), custom_call_target="tpu_custom_call" | custom-call | flops 1073741824 | bytes 4718592 | tf_op jit(solution)/shard_map/pallas_call | solution.py:31
  44.0 6.8 %collective-permute-done.1.cross_got_ref = bf16[256,256]{1,0:T(8,128)(2,1)S(1)} collective-permute-done((bf16[256,256]{1,0:T(8,128)(2,1)S(1)}, bf16[256,256]{1,0:T(8,128)(2,1)S(1)}, u32[]{:S(2)}, u32[]{:S(2)}) %collective-permute-start.1) | collective-permute-done | bytes 131104 | tf_op jit(solution)/shard_map/ppermute | solution.py:27
  50.8 0.0 collective-permute-done.9.got_ref
  50.8 1.0 %shard_map.102.rest_0_ = f32[256,2048]{1,0:T(8,128)} custom-call(s32[1]{0:T(128)S(6)} %copy.17.slot_ref, bf16[256,256]{1,0:T(8,128)(2,1)S(1)} %get-tuple-element.10.cross_ref, bf16[256,256]{1,0:T(8,128)(2,1)S(1)} %collective-permute-done.1.cross_got_ref, bf16[256,512]{1,0:T(8,128)(2,1)S(1)} %shard_map.101.sent_ref, ...), custom_call_target="tpu_custom_call" | custom-call | flops 67108864 | bytes 1048576 | tf_op jit(solution)/shard_map/pallas_call | solution.py:31
  51.8 0.0 collective-permute-done.8.got_ref
  51.8 1.0 %shard_map.103.rest_0_ = f32[256,2048]{1,0:T(8,128)} custom-call(s32[1]{0:T(128)S(6)} %copy.17.slot_ref, bf16[256,256]{1,0:T(8,128)(2,1)S(1)} %get-tuple-element.10.cross_ref, bf16[256,256]{1,0:T(8,128)(2,1)S(1)} %collective-permute-done.1.cross_got_ref, bf16[256,512]{1,0:T(8,128)(2,1)S(1)} %shard_map.100.sent_ref, ...), custom_call_target="tpu_custom_call", output_to_operand_aliasing={{}: (5, {})} | custom-call | flops 67108864 | bytes 1048576 | tf_op jit(solution)/shard_map/pallas_call | solution.py:31
  52.9 0.0 collective-permute-done.6.got_ref
  52.9 1.0 %shard_map.104.rest_0_ = f32[256,2048]{1,0:T(8,128)} custom-call(s32[1]{0:T(128)S(6)} %copy.17.slot_ref, bf16[256,256]{1,0:T(8,128)(2,1)S(1)} %get-tuple-element.10.cross_ref, bf16[256,256]{1,0:T(8,128)(2,1)S(1)} %collective-permute-done.1.cross_got_ref, bf16[256,512]{1,0:T(8,128)(2,1)S(1)} %shard_map.99.sent_ref, ...), custom_call_target="tpu_custom_call", output_to_operand_aliasing={{}: (5, {})} | custom-call | flops 67108864 | bytes 1048576 | tf_op jit(solution)/shard_map/pallas_call | solution.py:31
  53.9 0.0 collective-permute-done.4.got_ref
  53.9 1.0 %shard_map.105 = f32[256,2048]{1,0:T(8,128)} custom-call(s32[1]{0:T(128)S(6)} %copy.17.slot_ref, bf16[256,256]{1,0:T(8,128)(2,1)S(1)} %get-tuple-element.10.cross_ref, bf16[256,256]{1,0:T(8,128)(2,1)S(1)} %collective-permute-done.1.cross_got_ref, bf16[256,512]{1,0:T(8,128)(2,1)S(1)} %shard_map.98.sent_ref, ...), custom_call_target="tpu_custom_call", output_to_operand_aliasing={{}: (5, {})} | custom-call | flops 67108864 | bytes 1048576 | tf_op jit(solution)/shard_map/pallas_call | solution.py:31
  (8 shorter events, 0.1 us)
Async XLA Ops:
  1.9 2.2 %copy-start = (bf16[1024,2048]{1,0:T(8,128)(2,1)S(1)}, bf16[1024,2048]{1,0:T(8,128)(2,1)}, u32[]{:S(2)}) copy-start(bf16[1024,2048]{1,0:T(8,128)(2,1)} %tests_ref.13) | copy-start | bytes 12582916
  4.1 0.9 %copy-start.4 = (bf16[512,256]{1,0:T(8,128)(2,1)S(1)}, bf16[512,256]{1,0:T(8,128)(2,1)}, u32[]{:S(2)}) copy-start(bf16[512,256]{1,0:T(8,128)(2,1)} %coeffs_ref.11) | copy-start | bytes 786436
  5.1 1.6 %copy-start.6 = (bf16[512,2048]{1,0:T(8,128)(2,1)S(1)}, bf16[512,2048]{1,0:T(8,128)(2,1)}, u32[]{:S(2)}) copy-start(bf16[512,2048]{1,0:T(8,128)(2,1)} %samples_ref.3) | copy-start | bytes 6291460
  6.7 1.2 %copy-start.8 = (bf16[512,1024]{1,0:T(8,128)(2,1)S(1)}, bf16[512,1024]{1,0:T(8,128)(2,1)}, u32[]{:S(2)}) copy-start(bf16[512,1024]{1,0:T(8,128)(2,1)} %diag_ref.1) | copy-start | bytes 3145732
  7.9 0.9 %copy-start.9 = (bf16[256,256]{1,0:T(8,128)(2,1)S(1)}, bf16[256,256]{1,0:T(8,128)(2,1)}, u32[]{:S(2)}) copy-start(bf16[256,256]{1,0:T(8,128)(2,1)} %cross_ref.1) | copy-start | bytes 393220
  8.8 0.7 %copy-start.10 = (s32[1,256]{1,0:T(1,128)S(1)}, s32[1,256]{1,0:T(1,128)}, u32[]{:S(2)}) copy-start(s32[1,256]{1,0:T(1,128)} %skel_ref.11) | copy-start | bytes 3076
  9.5 4.5 %copy-start.1 = (bf16[1024,2048]{1,0:T(8,128)(2,1)S(1)}, bf16[1024,2048]{1,0:T(8,128)(2,1)}, u32[]{:S(2)}) copy-start(bf16[1024,2048]{1,0:T(8,128)(2,1)} %tests_ref.13) | copy-start | bytes 12582916
  9.5 4.5 %copy-start.7 = (bf16[512,2048]{1,0:T(8,128)(2,1)S(1)}, bf16[512,2048]{1,0:T(8,128)(2,1)}, u32[]{:S(2)}) copy-start(bf16[512,2048]{1,0:T(8,128)(2,1)} %samples_ref.3) | copy-start | bytes 6291460
  10.4 11.1 %collective-permute-start.2 = (bf16[512,256]{1,0:T(8,128)(2,1)S(1)}, bf16[512,256]{1,0:T(8,128)(2,1)S(1)}, u32[]{:S(2)}, u32[]{:S(2)}) collective-permute-start(bf16[512,256]{1,0:T(8,128)(2,1)S(1)} %get-tuple-element.11), channel_id=1, source_target_pairs={{0,1},{1,0},{2,3},{3,2},{4,5},{5,4},{6,7},{7,6},{8,9},{9,8},{10,11... | collective-permute-start | bytes 786440 | tf_op jit(solution)/shard_map/ppermute | solution.py:27
  14.0 6.7 %copy-start.5 = (bf16[512,256]{1,0:T(8,128)(2,1)S(1)}, bf16[512,256]{1,0:T(8,128)(2,1)}, u32[]{:S(2)}) copy-start(bf16[512,256]{1,0:T(8,128)(2,1)} %coeffs_ref.11) | copy-start | bytes 786436
  14.0 7.5 %copy-start.11 = (s32[1,256]{1,0:T(1,128)S(1)}, s32[1,256]{1,0:T(1,128)}, u32[]{:S(2)}) copy-start(s32[1,256]{1,0:T(1,128)} %skel_ref.11) | copy-start | bytes 3076
  17.3 9.4 %collective-permute-start.7 = (bf16[256,512]{1,0:T(8,128)(2,1)S(1)}, bf16[256,512]{1,0:T(8,128)(2,1)S(1)}, u32[]{:S(2)}, u32[]{:S(2)}) collective-permute-start(bf16[256,512]{1,0:T(8,128)(2,1)S(1)} %get-tuple-element.16.own_ref), channel_id=1, source_target_pairs={{0,1},{1,0},{2,3},{3,2},{4,5},{5,4},{6,7},{7,6},{8,9},{9,8},{10,11... | collective-permute-start | bytes 786440 | tf_op jit(solution)/shard_map/ppermute | solution.py:27
  18.6 13.7 %collective-permute-start.5 = (bf16[256,512]{1,0:T(8,128)(2,1)S(1)}, bf16[256,512]{1,0:T(8,128)(2,1)S(1)}, u32[]{:S(2)}, u32[]{:S(2)}) collective-permute-start(bf16[256,512]{1,0:T(8,128)(2,1)S(1)} %get-tuple-element.15.own_ref), channel_id=1, source_target_pairs={{0,1},{1,0},{2,3},{3,2},{4,5},{5,4},{6,7},{7,6},{8,9},{9,8},{10,11... | collective-permute-start | bytes 786440 | tf_op jit(solution)/shard_map/ppermute | solution.py:27
  19.4 18.6 %collective-permute-start.3 = (bf16[256,512]{1,0:T(8,128)(2,1)S(1)}, bf16[256,512]{1,0:T(8,128)(2,1)S(1)}, u32[]{:S(2)}, u32[]{:S(2)}) collective-permute-start(bf16[256,512]{1,0:T(8,128)(2,1)S(1)} %get-tuple-element.14.own_ref), channel_id=1, source_target_pairs={{0,1},{1,0},{2,3},{3,2},{4,5},{5,4},{6,7},{7,6},{8,9},{9,8},{10,11... | collective-permute-start | bytes 786440 | tf_op jit(solution)/shard_map/ppermute | solution.py:27
  20.7 20.1 %collective-permute-start = (bf16[512,128]{1,0:T(8,128)(2,1)S(1)}, bf16[512,128]{1,0:T(8,128)(2,1)S(1)}, u32[]{:S(2)}, u32[]{:S(2)}) collective-permute-start(bf16[512,128]{1,0:T(8,128)(2,1)S(1)} %constant_dynamic-slice_fusion), channel_id=1, source_target_pairs={{0,1},{1,0},{2,3},{3,2},{4,5},{5,4},{6,7},{7,6},{8,9},{9,8},{10,11... | collective-permute-start | bytes 393224 | tf_op jit(solution)/shard_map/ppermute | solution.py:27
  21.5 2.2 %copy-start.2 = (bf16[1024,2048]{1,0:T(8,128)(2,1)S(1)}, bf16[1024,2048]{1,0:T(8,128)(2,1)}, u32[]{:S(2)}) copy-start(bf16[1024,2048]{1,0:T(8,128)(2,1)} %tests_ref.13) | copy-start | bytes 12582916
  23.7 27.1 %collective-permute-start.9 = (bf16[256,512]{1,0:T(8,128)(2,1)S(1)}, bf16[256,512]{1,0:T(8,128)(2,1)S(1)}, u32[]{:S(2)}, u32[]{:S(2)}) collective-permute-start(bf16[256,512]{1,0:T(8,128)(2,1)S(1)} %shard_map.101.sent_ref), channel_id=1, source_target_pairs={{0,8},{8,0},{2,10},{10,2},{4,12},{12,4},{6,14},{14,6},{16,24},{24,... | collective-permute-start | bytes 786440 | tf_op jit(solution)/shard_map/ppermute | solution.py:27
  26.7 25.1 %collective-permute-start.8 = (bf16[256,512]{1,0:T(8,128)(2,1)S(1)}, bf16[256,512]{1,0:T(8,128)(2,1)S(1)}, u32[]{:S(2)}, u32[]{:S(2)}) collective-permute-start(bf16[256,512]{1,0:T(8,128)(2,1)S(1)} %shard_map.100.sent_ref), channel_id=1, source_target_pairs={{0,8},{8,0},{2,10},{10,2},{4,12},{12,4},{6,14},{14,6},{16,24},{24,... | collective-permute-start | bytes 786440 | tf_op jit(solution)/shard_map/ppermute | solution.py:27
  32.3 9.4 %copy-start.3 = (bf16[1024,2048]{1,0:T(8,128)(2,1)S(1)}, bf16[1024,2048]{1,0:T(8,128)(2,1)}, u32[]{:S(2)}) copy-start(bf16[1024,2048]{1,0:T(8,128)(2,1)} %tests_ref.13) | copy-start | bytes 12582916
  32.3 20.5 %collective-permute-start.6 = (bf16[256,512]{1,0:T(8,128)(2,1)S(1)}, bf16[256,512]{1,0:T(8,128)(2,1)S(1)}, u32[]{:S(2)}, u32[]{:S(2)}) collective-permute-start(bf16[256,512]{1,0:T(8,128)(2,1)S(1)} %shard_map.99.sent_ref), channel_id=1, source_target_pairs={{0,8},{8,0},{2,10},{10,2},{4,12},{12,4},{6,14},{14,6},{16,24},{24,... | collective-permute-start | bytes 786440 | tf_op jit(solution)/shard_map/ppermute | solution.py:27
  37.9 16.0 %collective-permute-start.4 = (bf16[256,512]{1,0:T(8,128)(2,1)S(1)}, bf16[256,512]{1,0:T(8,128)(2,1)S(1)}, u32[]{:S(2)}, u32[]{:S(2)}) collective-permute-start(bf16[256,512]{1,0:T(8,128)(2,1)S(1)} %shard_map.98.sent_ref), channel_id=1, source_target_pairs={{0,8},{8,0},{2,10},{10,2},{4,12},{12,4},{6,14},{14,6},{16,24},{24,... | collective-permute-start | bytes 786440 | tf_op jit(solution)/shard_map/ppermute | solution.py:27
  40.8 10.0 %collective-permute-start.1 = (bf16[256,256]{1,0:T(8,128)(2,1)S(1)}, bf16[256,256]{1,0:T(8,128)(2,1)S(1)}, u32[]{:S(2)}, u32[]{:S(2)}) collective-permute-start(bf16[256,256]{1,0:T(8,128)(2,1)S(1)} %get-tuple-element.10.cross_ref), channel_id=1, source_target_pairs={{0,8},{8,0},{2,10},{10,2},{4,12},{12,4},{6,14},{14,6},{16,24},{24,... | collective-permute-start | bytes 393224 | tf_op jit(solution)/shard_map/ppermute | solution.py:27
